TPU v7x, 32 devices: a whole 2x2x4 slice. The times are simulated.
32 devices in a mesh: layer: 4 (over y, x), feat: 8 (over z, core).
Axes of the slice: x: 2, y: 2, z: 4, core: 2. Of those that a mesh axis runs over, the one named last changes fastest.
Arguments:
- source_decoder: bfloat16 [4, 1024, 8192], P('layer', 'feat'), may hold values from -0.0625 to 0.0625
- reader_encoder: bfloat16 [4, 8192, 6144], P('layer', None, 'feat'), may hold values from -6 to 6
- source_acts: bfloat16 [2048, 4096], P('feat', 'layer'), may hold values from 0 to 2
- target_grads: bfloat16 [2048, 24576], P('feat', 'layer'), may hold values from -0.13183594 to 0.13183594
- pair_source: int32 [4, 8, 24], P('layer', 'feat'), may hold values from 0 to 3
- pair_target: int32 [4, 8, 24], P('layer', 'feat'), may hold values from 0 to 5
- pair_count: int32 [4, 8], P('layer', 'feat'), may hold values from 1 to 24, as said below
Outputs:
- edge_table: float32 [4, 8, 24, 128, 128], P('layer', 'feat')
Inputs may be any that keep to these rules, and one draw needn't show every extreme that they name: `pair_count`: slots at and past the count of a reader layer and column are unused; in every draw some reader layer and column uses all 24 slots.
All inputs are finite; a program needn't handle non-finite values.
Results may differ from a plain program's by a relative error of at most 0.0003.
Values may be sent and summed in bfloat16 or wider, within the bound.
A program may use at most 192 MiB of HBM per device.

v0:
```python
import jax
import jax.numpy as jnp
from jax import lax
from jax.sharding import PartitionSpec as P


def local(
    source_decoder, reader_encoder, source_acts, target_grads, pair_source, pair_target, pair_count
):
    source_rows, target_rows = (
        lax.all_to_all(source_acts, "feat", split_axis=1, concat_axis=0, tiled=True),
        lax.all_to_all(target_grads, "feat", split_axis=1, concat_axis=0, tiled=True),
    )
    encoder = reader_encoder[0]
    block_size = source_decoder.shape[1]
    source_slab = source_rows[None]
    sources = pair_source[0, 0]
    targets = pair_target[0, 0]
    slot_count = sources.shape[0]
    live_count = pair_count[0, 0]
    panel_dec, panel_act = (
        lax.all_gather(source_decoder, "layer", axis=0, tiled=True),
        lax.all_gather(source_slab, "layer", axis=0, tiled=True),
    )

    def one_pair(slot_pos, edge_buffer):
        source = sources[slot_pos]
        target = targets[slot_pos]
        decoder_block = lax.dynamic_index_in_dim(panel_dec, source, 0, keepdims=False)
        enc_block = lax.dynamic_slice_in_dim(encoder, target * block_size, block_size, 1)
        virtual = jnp.dot(decoder_block, enc_block, preferred_element_type=jnp.float32)
        act_block = lax.dynamic_index_in_dim(panel_act, source, 0, keepdims=False)
        grad_block = lax.dynamic_slice_in_dim(target_rows, target * block_size, block_size, 1)
        coact = lax.dot_general(
            act_block, grad_block, (((0,), (0,)), ((), ())), preferred_element_type=jnp.float32
        )
        return lax.dynamic_update_index_in_dim(edge_buffer, virtual * coact, slot_pos, 0)

    edge_table = lax.fori_loop(
        0, live_count, one_pair, jnp.zeros((slot_count, block_size, block_size), jnp.float32)
    )
    return edge_table[None, None]


def solution(mesh):
    in_specs = (
        P("layer", "feat", None),
        P("layer", None, "feat"),
        P("feat", "layer"),
        P("feat", "layer"),
        P("layer", "feat", None),
        P("layer", "feat", None),
        P("layer", "feat"),
    )
    out_specs = P("layer", "feat", None, None, None)
    return jax.shard_map(local, mesh=mesh, in_specs=in_specs, out_specs=out_specs, check_vma=False)
```

profile of v0, /device:TPU:5, one launch (start us, length us, event | category | flops | bytes accessed | tf_op | source)
XLA Modules:
  0.0 375.2 jit_solution(6197434539734011829)
XLA Ops:
  7.7 19.8 %all_to_all.35 = bf16[256,8,128]{2,0,1:T(8,128)(2,1)} all-to-all(bf16[256,8,128]{2,0,1:T(8,128)(2,1)S(1)} %copy_bitcast_fusion.1), channel_id=1, replica_groups=mesh['layer'=4,'feat'=8] {'feat'}, dimensions={1} | all-to-all | bytes 1048576 | tf_op jit(solution)/shard_map/all_to_all | solution.py:11
  28.2 3.8 %copy.16 = bf16[32,8,8,768]{3,2,0,1:T(8,128)(2,1)} copy(bf16[32,8,8,768]{3,2,1,0:T(8,128)(2,1)} %bitcast.44) | data formatting | bytes 6291456 | tf_op jit(solution)/shard_map/all_to_all | solution.py:12
  32.1 5.5 %all-to-all-start.1 = ((bf16[256,8,768]{2,0,1:T(8,128)(2,1)}), bf16[256,8,768]{2,0,1:T(8,128)(2,1)}, u32[]{:S(2)}, u32[]{:S(2)}) async-start(bf16[256,8,768]{2,0,1:T(8,128)(2,1)} %bitcast.42), calls=%async_computation.1 | async-start | bytes 6291456 | tf_op jit(solution)/shard_map/all_to_all | solution.py:12
  37.6 24.6 %all-gather.5.cloned.1.call-done = bf16[4,2048,128]{2,1,0:T(8,128)(2,1)} async-done(((bf16[1,2048,128]{2,1,0:T(8,128)(2,1)}), bf16[4,2048,128]{2,1,0:T(8,128)(2,1)}) %all-gather.5.cloned.1.call-update) | async-done | bytes 2097168 | tf_op jit(solution)/shard_map/all_gather | solution.py:23
  62.2 46.2 %all-to-all-done.1 = bf16[256,8,768]{2,0,1:T(8,128)(2,1)} async-done(((bf16[256,8,768]{2,0,1:T(8,128)(2,1)}), bf16[256,8,768]{2,0,1:T(8,128)(2,1)}, u32[]{:S(2)}, u32[]{:S(2)}) %all-to-all-start.1) | async-done | bytes 3145760 | tf_op jit(solution)/shard_map/all_to_all | solution.py:12
  108.4 43.3 %all-gather.3.cloned.1.call-done = bf16[4,128,8192]{2,1,0:T(8,128)(2,1)} async-done(((bf16[1,128,8192]{2,1,0:T(8,128)(2,1)}), bf16[4,128,8192]{2,1,0:T(8,128)(2,1)}) %all-gather.3.cloned.1.call-update) | async-done | bytes 8388624 | tf_op jit(solution)/shard_map/all_gather | solution.py:22
  151.8 215.3 %while.10 = (s32[]{:T(128)}, f32[24,128,128]{2,1,0:T(8,128)S(1)}, s32[]{:T(128)}, s32[24]{0:T(128)S(1)}, bf16[4,128,8192]{2,1,0:T(8,128)(2,1)}, /*index=5*/s32[2...) while((s32[]{:T(128)}, f32[24,128,128]{2,1,0:T(8,128)S(1)}, ...), condition=%wide.region_1.2_spmd, body=%wide.region_0.1_spmd.sunk | while | flops 335560704 | bytes 5439787 | solution.py:39
  156.3 2.9 fusion.22
  165.2 2.9 fusion.22
  174.2 2.9 fusion.22
  183.2 2.9 fusion.22
  192.1 2.9 fusion.22
  210.0 2.9 fusion.22
  218.9 2.9 fusion.22
  227.9 2.9 fusion.22
  236.8 2.9 fusion.22
  245.8 2.9 fusion.22
  254.7 2.9 fusion.22
  263.7 2.9 fusion.22
  272.6 2.9 fusion.22
  281.6 2.9 fusion.22
  299.4 2.9 fusion.22
  308.4 2.9 fusion.22
  317.3 2.9 fusion.22
  (93 shorter events, 92.0 us)
Async XLA Ops:
  6.5 1.0 copy-start
  6.5 55.6 %all-gather.5.cloned.1.call-start = ((), (), s32[]{:S(2)}) async-start(), calls=%async_computation.3 | async-start | bytes 2621440 | tf_op jit(solution)/shard_map/all_gather | solution.py:23
  27.5 124.2 %all-gather.3.cloned.1.call-start = ((), (), s32[]{:S(2)}) async-start(), calls=%async_computation.2 | async-start | bytes 10485760 | tf_op jit(solution)/shard_map/all_gather | solution.py:22
  32.0 119.8 %copy-start.2 = (s32[1,1,24]{2,1,0:T(1,128)S(1)}, s32[1,1,24]{2,1,0:T(1,128)}, u32[]{:S(2)}) copy-start(s32[1,1,24]{2,1,0:T(1,128)} %param.13) | copy-start | bytes 292
  32.1 119.8 %copy-start.3 = (s32[1,1,24]{2,1,0:T(1,128)S(1)}, s32[1,1,24]{2,1,0:T(1,128)}, u32[]{:S(2)}) copy-start(s32[1,1,24]{2,1,0:T(1,128)} %param.14) | copy-start | bytes 292
  32.1 76.3 %all-to-all-start.1 = ((bf16[256,8,768]{2,0,1:T(8,128)(2,1)}), bf16[256,8,768]{2,0,1:T(8,128)(2,1)}, u32[]{:S(2)}, u32[]{:S(2)}) async-start(bf16[256,8,768]{2,0,1:T(8,128)(2,1)} %bitcast.42), calls=%async_computation.1 | async-start | bytes 6291456 | tf_op jit(solution)/shard_map/all_to_all | solution.py:12
  367.2 1.1 copy-start.1
Sparse Core Ops, SparseCore 0:
  27.6 34.5 all-gather.4
  64.0 87.5 all-gather.2
where the time goes:
time: 377 us; the launch traced here: 375 us
  waiting for transfers between devices  115 us (31%)
  matrix products  107 us (28%)
  loops' own time  76.8 us (20%)
  local copies, waits for them, and re-layouts  37.4 us (10%)
  blocking collectives  19.8 us (5%)
  between operations  13.5 us (4%)
  starting transfers between devices  5.58 us (1%)
    another operation x1, loops' own time, local(): lax.fori_loop(0, live_count, one_pair, jnp.zeros((slot_count, block_size,...  76.8 us
    dot_general x24, matrix products, one_pair(): jnp.dot(decoder_block, enc_block, preferred_element_type=jnp.float32)  70.2 us
    all_to_all x1, waiting for transfers between devices, local(): lax.all_to_all(target_grads, 'feat', split_axis=1, concat_axis=0, tiled=T...  46.2 us
    all_gather x1, waiting for transfers between devices, local(): lax.all_gather(source_decoder, 'layer', axis=0, tiled=True)  43.3 us
    dot_general x24, matrix products, one_pair(): lax.dot_general(act_block, grad_block, (((0,), (0,)), ((), ())), preferre...  37.2 us
    all_gather x1, waiting for transfers between devices, local(): lax.all_gather(source_slab, 'layer', axis=0, tiled=True)  24.6 us
    all_to_all x1, blocking collectives, local(): lax.all_to_all(source_acts, 'feat', split_axis=1, concat_axis=0, tiled=True)  19.8 us
    dynamic_slice x24, local copies, waits for them, and re-layouts, one_pair(): target = targets[slot_pos]  15.6 us
  transfers between devices with their start and end apart: 3, of which 3 were waited for; matrix products, arithmetic and copies ran while one was open for 1% of the time, Pallas kernels for 0%

commit v1 on v0

--- a/solution.py
+++ b/solution.py
@@ -1,14 +1,27 @@
+import functools
 import jax
 import jax.numpy as jnp
 from jax import lax
 from jax.sharding import PartitionSpec as P
 
 
+def finish_the_wires(mat, row_axis, out_dim, which_dim):
+    w2 = lax.psum(1, axis_name=row_axis)
+    near = jnp.split(mat, w2, out_dim)
+    clean = jnp.stack(near)
+    part_next = lax.all_to_all(clean, row_axis, concat_axis=0, split_axis=0)
+    raw_out = jnp.concatenate(part_next, which_dim)
+    return raw_out
+
+
+_meet_group = functools.partial(finish_the_wires, row_axis="feat", out_dim=1, which_dim=0)
+
+
 def local(
     source_decoder, reader_encoder, source_acts, target_grads, pair_source, pair_target, pair_count
 ):
     source_rows, target_rows = (
-        lax.all_to_all(source_acts, "feat", split_axis=1, concat_axis=0, tiled=True),
+        _meet_group(source_acts),
         lax.all_to_all(target_grads, "feat", split_axis=1, concat_axis=0, tiled=True),
     )
     encoder = reader_encoder[0]

time: 377 us -> 386 us (1.024)
  matrix products: 107 us -> 119 us
  loops' own time: 76.8 us -> 70.9 us
    dot_general x24, matrix products: 37.2 us -> 48.6 us  [one_pair(): lax.dot_general(act_block, grad_block, (((0,), (0,)), ((), ())), preferre...]
    another operation x1, loops' own time: 76.8 us -> 70.9 us  [local(): lax.fori_loop(0, live_count, one_pair, jnp.zeros((slot_count, block_size,...]
    unnamed x8 -> x13, local copies, waits for them, and re-layouts: 2.18 us -> 6.13 us
where the time goes in v1:
time: 386 us; the launch traced here: 384 us
  matrix products  119 us (31%)
  waiting for transfers between devices  117 us (30%)
  loops' own time  70.9 us (18%)
  local copies, waits for them, and re-layouts  38.4 us (10%)
  blocking collectives  19.8 us (5%)
  between operations  13.4 us (3%)
  starting transfers between devices  4.78 us (1%)
    another operation x1, loops' own time, local(): lax.fori_loop(0, live_count, one_pair, jnp.zeros((slot_count, block_size,...  70.9 us
    dot_general x24, matrix products, one_pair(): jnp.dot(decoder_block, enc_block, preferred_element_type=jnp.float32)  70.2 us
    dot_general x24, matrix products, one_pair(): lax.dot_general(act_block, grad_block, (((0,), (0,)), ((), ())), preferre...  48.6 us
    all_gather x1, waiting for transfers between devices, local(): lax.all_gather(source_decoder, 'layer', axis=0, tiled=True)  46.1 us
    all_to_all x1, waiting for transfers between devices, local(): lax.all_to_all(target_grads, 'feat', split_axis=1, concat_axis=0, tiled=T...  43.4 us
    all_gather x1, waiting for transfers between devices, local(): lax.all_gather(source_slab, 'layer', axis=0, tiled=True)  27.3 us
    all_to_all x1, blocking collectives, finish_the_wires(): part_next = lax.all_to_all(clean, row_axis, concat_axis=0, split_axis=0)  19.8 us
    dynamic_slice x24, local copies, waits for them, and re-layouts, one_pair(): target = targets[slot_pos]  14.1 us
  transfers between devices with their start and end apart: 3, of which 3 were waited for; matrix products, arithmetic and copies ran while one was open for 1% of the time, Pallas kernels for 0%

profile of v1, /device:TPU:5, one launch (start us, length us, event | category | flops | bytes accessed | tf_op | source)
XLA Modules:
  0.0 383.6 jit_solution(13111793089587479525)
XLA Ops:
  13.5 19.8 %all_to_all.24 = bf16[8,256,128]{2,1,0:T(8,128)(2,1)} all-to-all(bf16[8,256,128]{2,1,0:T(8,128)(2,1)S(1)} %bitcast_dynamic-update-slice_fusion), channel_id=1, replica_groups=mesh['layer'=4,'feat'=8] {'feat'}, dimensions={0} | all-to-all | bytes 1048576 | tf_op jit(solution)/shard_map/all_to_all | solution.py:12
  36.0 4.7 %all-to-all-start.1 = ((bf16[256,8,768]{2,0,1:T(8,128)(2,1)}), bf16[256,8,768]{2,0,1:T(8,128)(2,1)S(1)}, u32[]{:S(2)}, u32[]{:S(2)}) async-start(bf16[256,8,768]{2,0,1:T(8,128)(2,1)} %bitcast.40), calls=%async_computation.1 | async-start | bytes 6291456 | tf_op jit(solution)/shard_map/all_to_all | solution.py:25
  40.8 27.3 %all-gather.5.cloned.1.call-done = bf16[4,2048,128]{2,1,0:T(8,128)(2,1)} async-done(((bf16[1,2048,128]{2,1,0:T(8,128)(2,1)}), bf16[4,2048,128]{2,1,0:T(8,128)(2,1)}) %all-gather.5.cloned.1.call-update) | async-done | bytes 2097168 | tf_op jit(solution)/shard_map/all_gather | solution.py:36
  68.0 43.4 %all-to-all-done.1 = bf16[256,8,768]{2,0,1:T(8,128)(2,1)S(1)} async-done(((bf16[256,8,768]{2,0,1:T(8,128)(2,1)}), bf16[256,8,768]{2,0,1:T(8,128)(2,1)S(1)}, u32[]{:S(2)}, u32[]{:S(2)}) %all-to-all-start.1) | async-done | bytes 3145760 | tf_op jit(solution)/shard_map/all_to_all | solution.py:25
  111.4 46.1 %all-gather.3.cloned.1.call-done = bf16[4,128,8192]{2,1,0:T(8,128)(2,1)} async-done(((bf16[1,128,8192]{2,1,0:T(8,128)(2,1)}), bf16[4,128,8192]{2,1,0:T(8,128)(2,1)}) %all-gather.3.cloned.1.call-update) | async-done | bytes 8388624 | tf_op jit(solution)/shard_map/all_gather | solution.py:35
  158.8 218.0 %while.10 = (s32[]{:T(128)}, f32[24,128,128]{2,1,0:T(8,128)}, s32[]{:T(128)}, s32[24]{0:T(128)S(1)}, bf16[4,128,8192]{2,1,0:T(8,128)(2,1)}, /*index=5*/s32[24]{0...) while((s32[]{:T(128)}, f32[24,128,128]{2,1,0:T(8,128)}, ...), condition=%wide.region_1.2_spmd, body=%wide.region_0.1_spmd.sunk | while | flops 335560704 | bytes 5439787 | solution.py:52
  162.9 2.9 fusion.21
  172.0 2.9 fusion.21
  181.0 2.9 fusion.21
  190.1 2.9 fusion.21
  199.1 2.9 fusion.21
  208.2 2.9 fusion.21
  217.2 2.9 fusion.21
  226.3 2.9 fusion.21
  244.4 2.9 fusion.21
  253.5 2.9 fusion.21
  271.6 2.9 fusion.21
  289.7 2.9 fusion.21
  298.7 2.9 fusion.21
  316.8 2.9 fusion.21
  325.9 2.9 fusion.21
  344.0 2.9 fusion.21
  353.1 2.9 fusion.21
  371.2 2.9 fusion.21
  (98 shorter events, 105.4 us)
Async XLA Ops:
  6.5 61.5 %all-gather.5.cloned.1.call-start = ((), (), s32[]{:S(2)}) async-start(), calls=%async_computation.3 | async-start | bytes 2621440 | tf_op jit(solution)/shard_map/all_gather | solution.py:36
  9.9 24.1 %copy-start = (bf16[256,6144]{1,0:T(8,128)(2,1)S(1)}, bf16[256,6144]{1,0:T(8,128)(2,1)}, u32[]{:S(2)}) copy-start(bf16[256,6144]{1,0:T(8,128)(2,1)} %param.12) | copy-start | bytes 9437188
  33.3 124.2 %all-gather.3.cloned.1.call-start = ((), (), s32[]{:S(2)}) async-start(), calls=%async_computation.2 | async-start | bytes 10485760 | tf_op jit(solution)/shard_map/all_gather | solution.py:35
  36.0 122.8 %copy-start.1 = (s32[1,1,24]{2,1,0:T(1,128)S(1)}, s32[1,1,24]{2,1,0:T(1,128)}, u32[]{:S(2)}) copy-start(s32[1,1,24]{2,1,0:T(1,128)} %param.13) | copy-start | bytes 292
  36.0 122.8 %copy-start.2 = (s32[1,1,24]{2,1,0:T(1,128)S(1)}, s32[1,1,24]{2,1,0:T(1,128)}, u32[]{:S(2)}) copy-start(s32[1,1,24]{2,1,0:T(1,128)} %param.14) | copy-start | bytes 292
  36.0 75.4 %all-to-all-start.1 = ((bf16[256,8,768]{2,0,1:T(8,128)(2,1)}), bf16[256,8,768]{2,0,1:T(8,128)(2,1)S(1)}, u32[]{:S(2)}, u32[]{:S(2)}) async-start(bf16[256,8,768]{2,0,1:T(8,128)(2,1)} %bitcast.40), calls=%async_computation.1 | async-start | bytes 6291456 | tf_op jit(solution)/shard_map/all_to_all | solution.py:25
Sparse Core Ops, SparseCore 0:
  33.4 34.5 all-gather.4
  69.8 87.5 all-gather.2
